TPU v7x, 32 devices: a whole 2x2x4 slice. The times are simulated.
32 devices in a mesh: grp: 2 (over y), row: 8 (over z, x), col: 2 (over core).
Axes of the slice: x: 2, y: 2, z: 4, core: 2. Of those that a mesh axis runs over, the one named last changes fastest.
Arguments:
- images: bfloat16 [256, 768], P(('grp', 'row', 'col')), parts along dimension 0, may hold values from -0.5 to 0.5
- texts: bfloat16 [256, 768], P(('grp', 'row', 'col')), parts along dimension 0, may hold values from -0.5 to 0.5
- match: int32 [256], P(('grp', 'row', 'col')), parts along dimension 0, may hold values from 0 to 127, as said below
- logit_scale: float32 [1], replicated, may hold values from 6 to 12
- logit_bias: float32 [1], replicated, may hold values from -9 to -6
Outputs:
- loss: float32 [2], P('grp'), parts along dimension 0
- grad_images: float32 [256, 768], P(('grp', 'row', 'col')), parts along dimension 0
- grad_texts: float32 [256, 768], P(('grp', 'row', 'col')), parts along dimension 0
There are 2 independent parts, one for each index of `grp`. A program takes and returns all parts, laid end to end along the dimension named above; an argument that names none is the same for every part. Nothing has to cross between parts.
Inputs may be any that keep to these rules, and one draw needn't show every extreme that they name: match is a permutation of 0 to 127.
All inputs are finite; a program needn't handle non-finite values.
Results may differ from a plain program's by a relative error of at most 0.0051.
Values may be sent and summed in bfloat16 or wider, within the bound.
A program may use at most 64 MiB of HBM per device.

v0:
```python
import jax
import jax.numpy as jnp
from jax import lax
from jax.sharding import PartitionSpec as P


def unit_rows(values):
    wide = values.astype(jnp.float32)
    norms = jnp.sqrt(jnp.sum(wide * wide, axis=1, keepdims=True) + 1e-06)
    return (wide / norms, norms)


def back_rows(unit, norms, grads):
    inner = jnp.sum(unit * grads, axis=1, keepdims=True)
    return (grads - unit * inner) / norms


def body(images, texts, match, logit_scale, logit_bias):
    scale = logit_scale[0]
    offset = logit_bias[0]
    shard = images.shape[0]
    row_count = lax.axis_size("row")
    col_count = lax.axis_size("col")
    unit_img, inorm = unit_rows(images)
    unit_txt, tnorm = unit_rows(texts)
    img_b = unit_img.astype(jnp.bfloat16)
    txt_b = unit_txt.astype(jnp.bfloat16)
    img_block, match_block = (
        lax.all_gather(img_b, "col", axis=0, tiled=True),
        lax.all_gather(match, "col", axis=0, tiled=True),
    )
    txt_block = lax.all_gather(txt_b, "row", axis=0, tiled=True)
    width = txt_block.shape[0]
    local = jnp.arange(width, dtype=jnp.int32)
    owner = local // shard
    text_index = (owner * col_count + lax.axis_index("col")) * shard + local % shard
    logits = (
        scale
        * lax.dot_general(
            img_block, txt_block, (((1,), (1,)), ((), ())), preferred_element_type=jnp.float32
        )
        + offset
    )
    label = jnp.where(
        match_block[:, None] == text_index[None, :], jnp.float32(1.0), jnp.float32(-1.0)
    )
    partial_loss = jnp.sum(jax.nn.log_sigmoid(label * logits))
    total = lax.psum(partial_loss, ("row", "col"))
    loss = (-total / (shard * row_count * col_count)).reshape(1)
    coef = (-label * jax.nn.sigmoid(-label * logits)).astype(jnp.bfloat16)
    img_terms = jnp.dot(coef, txt_block, preferred_element_type=jnp.float32)
    gimg = scale * lax.psum_scatter(img_terms, "col", scatter_dimension=0, tiled=True)
    txt_terms = lax.dot_general(
        coef, img_block, (((0,), (0,)), ((), ())), preferred_element_type=jnp.float32
    )
    gtxt = scale * lax.psum_scatter(txt_terms, "row", scatter_dimension=0, tiled=True)
    return (loss, back_rows(unit_img, inorm, gimg), back_rows(unit_txt, tnorm, gtxt))


def solution(mesh):
    placed = (
        P(("grp", "row", "col"), None),
        P(("grp", "row", "col"), None),
        P(("grp", "row", "col")),
        P(),
        P(),
    )
    return jax.shard_map(
        body,
        mesh=mesh,
        in_specs=placed,
        out_specs=(P("grp"), P(("grp", "row", "col"), None), P(("grp", "row", "col"), None)),
        check_vma=False,
    )
```

profile of v0, /device:TPU:0, one launch (start us, length us, event | category | flops | bytes accessed | tf_op | source)
XLA Modules:
  0.0 132.9 jit_solution(3644196438063744677)
XLA Ops:
  7.2 0.0 copy-start
  7.2 0.0 reduce-scatter.3.cloned.1.call-start
  7.2 0.0 copy-start.1
  8.6 0.0 copy-done
  8.6 0.1 fusion.1
  8.7 0.0 copy-done.1
  8.7 0.1 fusion.2
  8.8 0.0 copy-start.5
  8.8 0.6 copy-done.5
  9.5 0.6 dynamic-slice
  10.7 0.0 copy-start.4
  10.7 0.6 copy-done.4
  11.4 0.2 dynamic-update-slice
  11.6 1.9 %all-reduce = s32[16]{0:T(128)S(1)} all-reduce(s32[16]{0:T(128)S(1)} %dynamic-update-slice), channel_id=1, replica_groups=mesh['grp'=2,'row'=8,'col'=2] {'col'}, use_global_device_ids=true, to_apply=%add | all-reduce | flops 16 | bytes 128
  13.5 0.1 fusion.17
  13.6 0.1 fusion.16
  13.6 1.8 %all_gather.10 = bf16[16,768]{1,0:T(8,128)(2,1)S(1)} all-gather(bf16[8,768]{1,0:T(8,128)(2,1)S(1)} %fusion.16), channel_id=1, replica_groups=mesh['grp'=2,'row'=8,'col'=2] {'col'}, dimensions={0}, use_global_device_ids=true | all-gather | bytes 36864 | tf_op jit(solution)/shard_map/all_gather | solution.py:29
  15.5 32.2 %all_gather.11 = bf16[64,768]{1,0:T(8,128)(2,1)S(1)} all-gather(bf16[8,768]{1,0:T(8,128)(2,1)S(1)} %fusion.17), channel_id=1, replica_groups=mesh['grp'=2,'row'=8,'col'=2] {'row'}, dimensions={0}, use_global_device_ids=true | all-gather | bytes 110592 | tf_op jit(solution)/shard_map/all_gather | solution.py:32
  47.7 0.8 fusion.10
  48.4 0.8 fusion.20
  49.3 0.0 reduce-scatter.3.cloned.1.call-update
  49.3 0.0 reduce-scatter.5.cloned.1.call-start
  49.3 1.0 fusion.18
  50.3 0.0 reduce-scatter.5.cloned.1.call-update
  51.0 30.0 %psum.7 = f32[]{:T(128)} all-reduce(f32[]{:T(128)S(6)} %neg.25), channel_id=1, replica_groups=mesh['grp'=2,'row'=8,'col'=2] {'row','col'}, use_global_device_ids=true, to_apply=%region_3.4 | all-reduce | flops 1 | bytes 8 | tf_op jit(solution)/shard_map/psum | solution.py:48
  81.6 0.0 reduce-scatter.3.cloned.1.call-done
  81.7 0.0 copy-start.2
  81.7 1.0 multiply_reduce_fusion.1
  82.7 0.0 copy-done.2
  82.7 0.7 subtract_divide_fusion.1
  83.4 39.9 %reduce-scatter.5.cloned.1.call-done = f32[8,768]{1,0:T(8,128)} async-done(((f32[64,768]{1,0:T(8,128)}), f32[8,768]{1,0:T(8,128)}) %reduce-scatter.5.cloned.1.call-update) | async-done | bytes 24592 | tf_op jit(solution)/shard_map/reduce_scatter | solution.py:56
  123.2 0.0 copy-start.3
  123.2 1.0 multiply_reduce_fusion
  124.2 0.0 copy-done.3
  124.2 0.7 subtract_divide_fusion
  (4 shorter events, 0.0 us)
Async XLA Ops:
  7.2 1.4 %copy-start = (bf16[8,768]{1,0:T(8,128)(2,1)S(1)}, bf16[8,768]{1,0:T(8,128)(2,1)}, u32[]{:S(2)}) copy-start(bf16[8,768]{1,0:T(8,128)(2,1)} %param.5) | copy-start | bytes 36868
  7.2 74.5 %reduce-scatter.3.cloned.1.call-start = ((), (), s32[]{:S(2)}) async-start(), calls=%async_computation.2 | async-start | bytes 73728 | tf_op jit(solution)/shard_map/reduce_scatter | solution.py:52
  7.2 1.5 %copy-start.1 = (bf16[8,768]{1,0:T(8,128)(2,1)S(1)}, bf16[8,768]{1,0:T(8,128)(2,1)}, u32[]{:S(2)}) copy-start(bf16[8,768]{1,0:T(8,128)(2,1)} %param.6) | copy-start | bytes 36868
  8.8 0.7 copy-start.5
  10.7 0.7 copy-start.4
  49.3 73.9 %reduce-scatter.5.cloned.1.call-start = ((), (), s32[]{:S(2)}) async-start(), calls=%async_computation.3 | async-start | bytes 221184 | tf_op jit(solution)/shard_map/reduce_scatter | solution.py:56
  81.7 1.0 copy-start.2
  123.2 1.0 copy-start.3
Sparse Core Ops, SparseCore 0:
  49.4 8.3 reduce-scatter.2
  61.0 62.1 reduce-scatter.4
where the time goes:
time: 133 us
  blocking collectives  66 us (50%)
  waiting for transfers between devices  39.9 us (30%)
  between operations  18.5 us (14%)
  other arithmetic  3.77 us (3%)
  matrix products  2.56 us (2%)
  local copies, waits for them, and re-layouts  2.06 us (2%)
    reduce_scatter x1, waiting for transfers between devices, body(): lax.psum_scatter(txt_terms, 'row', scatter_dimension=0, tiled=True)  39.9 us
    all_gather x1, blocking collectives, body(): txt_block = lax.all_gather(txt_b, 'row', axis=0, tiled=True)  32.2 us
    psum x1, blocking collectives, body(): total = lax.psum(partial_loss, ('row', 'col'))  30 us
  transfers between devices with their start and end apart: 2, of which 1 were waited for; matrix products, arithmetic and copies ran while one was open for 2% of the time, Pallas kernels for 0%

commit v1 on v0

v1 whole, which is shorter than its diff:
```python
import functools
import jax
import jax.numpy as jnp
from jax import lax
from jax.experimental import pallas as pl
from jax.experimental.pallas import tpu as pltpu
from jax.sharding import PartitionSpec as P

MESH = pl.DeviceIdType.MESH
F32 = jnp.float32
BF16 = jnp.bfloat16


def split_rows(row_count, col_count):
    best = 1
    for low in range(1, row_count + 1):
        if row_count % low == 0:
            if max(low * col_count, row_count // low) < max(best * col_count, row_count // best):
                best = low
    return best


def unit_rows(values):
    wide = values.astype(F32)
    norms = jnp.sqrt(jnp.sum(wide * wide, axis=1, keepdims=True) + 1e-06)
    return (wide / norms, norms)


def back_rows(unit, norms, grads):
    inner = jnp.sum(unit * grads, axis=1, keepdims=True)
    return (grads - unit * inner) / norms


def fold(rows):
    half = rows.shape[1] // 2
    return jnp.concatenate([rows[:, :half], rows[:, half:]], axis=0)


def unfold(blocks):
    n, r2, h = blocks.shape
    r = r2 // 2
    wide = blocks.astype(F32)
    left = wide[:, :r, :].reshape(n * r, h)
    right = wide[:, r:, :].reshape(n * r, h)
    return jnp.concatenate([left, right], axis=1)


def kernel(
    low,
    row_count,
    col_count,
    images_hbm,
    texts_hbm,
    match_hbm,
    scale_hbm,
    bias_hbm,
    loss_ref,
    gimg_ref,
    gtxt_ref,
    images_ref,
    texts_ref,
    match_ref,
    scale_ref,
    bias_ref,
    img_buf,
    txt_buf,
    match_buf,
    img_part,
    txt_part,
    img_back,
    txt_back,
    loss_own,
    loss_buf,
    in_sem,
    img_send,
    img_recv,
    txt_send,
    txt_recv,
    match_send,
    match_recv,
    ipart_send,
    ipart_recv,
    tpart_send,
    tpart_recv,
    loss_send,
    loss_recv,
):
    shard, width = images_ref.shape
    high = row_count // low
    wide = low * col_count
    count = row_count * col_count
    row = lax.axis_index("row")
    col = lax.axis_index("col")
    hi, lo = row // low, row % low
    place = lo * col_count + col

    def at_place(q):
        return {"row": hi * low + q // col_count, "col": q % col_count}

    def at_high(p):
        return {"row": p * low + lo, "col": col}

    loads = [
        pltpu.make_async_copy(src, dst, in_sem.at[n])
        for n, (src, dst) in enumerate(
            [
                (images_hbm, images_ref),
                (texts_hbm, texts_ref),
                (match_hbm, match_ref),
                (scale_hbm, scale_ref),
                (bias_hbm, bias_ref),
            ]
        )
    ]
    for load in loads:
        load.start()

    barrier = pltpu.get_barrier_semaphore()
    for o in range(1, high):
        pl.semaphore_signal(barrier, inc=1, device_id=at_high((hi + o) % high), device_id_type=MESH)
    for o in range(1, wide):
        pl.semaphore_signal(barrier, inc=1, device_id=at_place((place + o) % wide), device_id_type=MESH)

    for load in loads:
        load.wait()
    unit_txt, tnorm = unit_rows(texts_ref[...])
    unit_img, inorm = unit_rows(images_ref[...])
    txt_buf[0] = fold(unit_txt).astype(BF16)
    img_buf[0] = fold(unit_img).astype(BF16)
    sub = lax.broadcasted_iota(jnp.int32, (shard, 128), 0)
    own_match = jnp.zeros((shard, 128), jnp.int32)
    for r in range(shard):
        own_match = jnp.where(sub == r, match_ref[r], own_match)
    match_buf[0] = own_match
    scale = scale_ref[0]
    offset = bias_ref[0]

    pl.semaphore_wait(barrier, high + wide - 2)

    first = []
    for o in range(1, high):
        first.append(
            pltpu.make_async_remote_copy(
                txt_buf.at[0], txt_buf.at[o], txt_send.at[o], txt_recv.at[o],
                device_id=at_high((hi + o) % high), device_id_type=MESH,
            )
        )
    for o in range(1, wide):
        target = at_place((place + o) % wide)
        first.append(
            pltpu.make_async_remote_copy(
                img_buf.at[0], img_buf.at[o], img_send.at[o], img_recv.at[o],
                device_id=target, device_id_type=MESH,
            )
        )
        first.append(
            pltpu.make_async_remote_copy(
                match_buf.at[0], match_buf.at[o], match_send.at[o], match_recv.at[o],
                device_id=target, device_id_type=MESH,
            )
        )
    for copy in first:
        copy.start()
    for copy in first:
        copy.wait_recv()

    img_block = unfold(img_buf[...]).astype(BF16)
    txt_block = unfold(txt_buf[...]).astype(BF16)
    rows, cols = wide * shard, high * shard
    lane = lax.broadcasted_iota(jnp.int32, (rows, cols), 1)
    source = hi - lane // shard
    source = jnp.where(source < 0, source + high, source)
    text_index = (source * wide + place) * shard + lane % shard
    match_block = match_buf[...].reshape(rows, 128)[:, :1]
    label = jnp.where(match_block == text_index, F32(1.0), F32(-1.0))
    logits = (
        scale
        * lax.dot_general(img_block, txt_block, (((1,), (1,)), ((), ())), preferred_element_type=F32)
        + offset
    )
    signed = label * logits
    decay = jnp.exp(-jnp.abs(signed))
    terms = jnp.minimum(signed, 0.0) - jnp.log1p(decay)
    coef = (-label * jnp.where(signed >= 0, decay, 1.0) / (1.0 + decay)).astype(BF16)

    loss_own[...] = jnp.full(loss_own.shape, jnp.sum(terms), F32)

    def loss_copy(o):
        p = place + o % wide
        p = jnp.where(p >= wide, p - wide, p)
        h = hi + o // wide
        h = jnp.where(h >= high, h - high, h)
        target = {"row": h * low + p // col_count, "col": p % col_count}
        return pltpu.make_async_remote_copy(
            loss_own, loss_buf.at[o], loss_send.at[o], loss_recv.at[o],
            device_id=target, device_id_type=MESH,
        )

    second = []
    txt_terms = lax.dot_general(coef, img_block, (((0,), (0,)), ((), ())), preferred_element_type=F32)
    txt_part[...] = txt_terms.reshape(high, shard, width)
    for o in range(1, high):
        second.append(
            pltpu.make_async_remote_copy(
                txt_part.at[o], txt_back.at[o], tpart_send.at[o], tpart_recv.at[o],
                device_id=at_high((hi + high - o) % high), device_id_type=MESH,
            )
        )
        second[-1].start()
    img_terms = jnp.dot(coef, txt_block, preferred_element_type=F32)
    img_part[...] = img_terms.reshape(wide, shard, width)
    for o in range(1, wide):
        second.append(
            pltpu.make_async_remote_copy(
                img_part.at[o], img_back.at[o], ipart_send.at[o], ipart_recv.at[o],
                device_id=at_place((place + wide - o) % wide), device_id_type=MESH,
            )
        )
        second[-1].start()

    if count <= 32:
        for o in range(1, count):
            loss_copy(o).start()
    else:
        lax.fori_loop(1, count, lambda o, c: (loss_copy(o).start(), c)[1], 0)

    for copy in second:
        copy.wait_recv()
    gimg = img_part[0]
    for o in range(1, wide):
        gimg = gimg + img_back[o]
    gimg_ref[...] = back_rows(unit_img, inorm, scale * gimg)
    gtxt = txt_part[0]
    for o in range(1, high):
        gtxt = gtxt + txt_back[o]
    gtxt_ref[...] = back_rows(unit_txt, tnorm, scale * gtxt)

    loss_buf[0] = loss_own[...]
    if count <= 32:
        for o in range(1, count):
            loss_copy(o).wait_recv()
    else:
        lax.fori_loop(1, count, lambda o, c: (loss_copy(o).wait_recv(), c)[1], 0)
    total = jnp.sum(loss_buf[...], axis=0)
    loss_ref[0] = -total[0, 0] / (shard * count)

    for copy in first + second:
        copy.wait_send()
    if count <= 32:
        for o in range(1, count):
            loss_copy(o).wait_send()
    else:
        lax.fori_loop(1, count, lambda o, c: (loss_copy(o).wait_send(), c)[1], 0)


def body(images, texts, match, logit_scale, logit_bias):
    row_count = lax.axis_size("row")
    col_count = lax.axis_size("col")
    low = split_rows(row_count, col_count)
    high = row_count // low
    wide = low * col_count
    count = row_count * col_count
    shard, width = images.shape
    dma = pltpu.SemaphoreType.DMA
    return tuple(
        pl.pallas_call(
            functools.partial(kernel, low, row_count, col_count),
            out_shape=(
                jax.ShapeDtypeStruct((1,), F32),
                jax.ShapeDtypeStruct((shard, width), F32),
                jax.ShapeDtypeStruct((shard, width), F32),
            ),
            in_specs=[pl.BlockSpec(memory_space=pl.ANY)] * 5,
            out_specs=(
                pl.BlockSpec(memory_space=pltpu.SMEM),
                pl.BlockSpec(memory_space=pltpu.VMEM),
                pl.BlockSpec(memory_space=pltpu.VMEM),
            ),
            scratch_shapes=[
                pltpu.VMEM((shard, width), BF16),
                pltpu.VMEM((shard, width), BF16),
                pltpu.SMEM((shard,), jnp.int32),
                pltpu.SMEM((1,), F32),
                pltpu.SMEM((1,), F32),
                pltpu.VMEM((wide, 2 * shard, width // 2), BF16),
                pltpu.VMEM((high, 2 * shard, width // 2), BF16),
                pltpu.VMEM((wide, shard, 128), jnp.int32),
                pltpu.VMEM((wide, shard, width), F32),
                pltpu.VMEM((high, shard, width), F32),
                pltpu.VMEM((wide, shard, width), F32),
                pltpu.VMEM((high, shard, width), F32),
                pltpu.VMEM((8, 128), F32),
                pltpu.VMEM((count, 8, 128), F32),
                dma((5,)),
                dma((wide,)),
                dma((wide,)),
                dma((high,)),
                dma((high,)),
                dma((wide,)),
                dma((wide,)),
                dma((wide,)),
                dma((wide,)),
                dma((high,)),
                dma((high,)),
                dma((count,)),
                dma((count,)),
            ],
            compiler_params=pltpu.CompilerParams(
                collective_id=0, has_side_effects=True, vmem_limit_bytes=32 * 1024 * 1024
            ),
        )(images, texts, match, logit_scale, logit_bias)
    )


def solution(mesh):
    placed = (
        P(("grp", "row", "col"), None),
        P(("grp", "row", "col"), None),
        P(("grp", "row", "col")),
        P(),
        P(),
    )
    return jax.shard_map(
        body,
        mesh=mesh,
        in_specs=placed,
        out_specs=(P("grp"), P(("grp", "row", "col"), None), P(("grp", "row", "col"), None)),
        check_vma=False,
    )
```

time: 133 us -> 22.6 us (0.17)
  blocking collectives: 66 us -> 0 us
  waiting for transfers between devices: 39.9 us -> 0 us
  Pallas kernels: 0 us -> 15.9 us
  between operations: 18.5 us -> 3.71 us
  other arithmetic: 3.77 us -> 0 us
  matrix products: 2.56 us -> 0 us
    reduce_scatter x2 -> x0, waiting for transfers between devices: 39.9 us -> none  [the longest x1 39.9 us: body(): lax.psum_scatter(txt_terms, 'row', scatter_dimension=0, tiled=True)]
    all_gather x2 -> x0, blocking collectives: 34 us -> none  [the longest x1 32.2 us: body(): txt_block = lax.all_gather(txt_b, 'row', axis=0, tiled=True)]
    psum x1 -> x0, blocking collectives: 30 us -> none  [body(): total = lax.psum(partial_loss, ('row', 'col'))]
    pallas_call x0 -> x1, Pallas kernels: none -> 15.9 us  [body(): pl.pallas_call(functools.partial(kernel, low, row_count, col_count), out_...]
    dot_general x3 -> x0, matrix products: 2.56 us -> none  [the longest x1 0.96 us: body(): lax.dot_general(coef, img_block, (((0,), (0,)), ((), ())), preferred_elem...]
    reduce_sum x4 -> x0, other arithmetic: 2.22 us -> none  [the longest x2 1.98 us: back_rows(): inner = jnp.sum(unit * grads, axis=1, keepdims=True)]
    unnamed x1 -> x0, blocking collectives: 1.92 us -> none
    div x2 -> x0, other arithmetic: 1.38 us -> none  [back_rows(): return (grads - unit * inner) / norms]
  transfers between devices with their start and end apart: 2 -> 0, of which waited for: 1 -> 0; matrix products, arithmetic and copies ran while one was open for 2% -> 0% of each run, Pallas kernels for 0% -> 0%
where the time goes in v1:
time: 22.6 us; the launch traced here: 22.2 us
  Pallas kernels  15.9 us (70%)
  between operations  3.71 us (16%)
  local copies, waits for them, and re-layouts  2.63 us (12%)
    pallas_call x1, Pallas kernels, body(): pl.pallas_call(functools.partial(kernel, low, row_count, col_count), out_...  15.9 us
    unnamed x8, local copies, waits for them, and re-layouts  2.63 us

profile of v1, /device:TPU:0, one launch (start us, length us, event | category | flops | bytes accessed | tf_op | source)
XLA Modules:
  0.0 22.2 jit_solution(15649909308776489228)
XLA Ops:
  1.3 0.0 copy-start.2
  1.9 0.0 copy-done.2
  2.0 0.0 copy-start
  2.0 0.7 %copy-done = bf16[8,768]{1,0:T(8,128)(2,1)S(1)} copy-done((bf16[8,768]{1,0:T(8,128)(2,1)S(1)}, bf16[8,768]{1,0:T(8,128)(2,1)}, u32[]{:S(2)}) %copy-start) | copy-done | bytes 12312
  2.7 0.0 copy-start.1
  2.7 0.7 %copy-done.1 = bf16[8,768]{1,0:T(8,128)(2,1)S(1)} copy-done((bf16[8,768]{1,0:T(8,128)(2,1)S(1)}, bf16[8,768]{1,0:T(8,128)(2,1)}, u32[]{:S(2)}) %copy-start.1) | copy-done | bytes 12312
  3.4 15.9 %shard_map.76 = (f32[1]{0:T(128)}, f32[8,768]{1,0:T(8,128)S(1)}, f32[8,768]{1,0:T(8,128)S(1)}) custom-call(bf16[8,768]{1,0:T(8,128)(2,1)S(1)} %copy-done, bf16[8,768]{1,0:T(8,128)(2,1)S(1)} %copy-done.1, s32[8]{0:T(128)S(1)} %copy-done.2, f32[1]{0:T(128)S(6)} %copy.11.scale_hbm, f32[1]{0:T(128)S(6)} %copy.12.bias_hbm), custom_call_target="tpu_custom_call" | custom-call | tf_op jit(solution)/shard_map/pallas_call | solution.py:266
  19.9 0.6 %copy.14 = f32[8,768]{1,0:T(8,128)} copy(f32[8,768]{1,0:T(8,128)S(1)} %get-tuple-element.7) | data formatting | bytes 49152
  20.5 0.6 %copy.15 = f32[8,768]{1,0:T(8,128)} copy(f32[8,768]{1,0:T(8,128)S(1)} %get-tuple-element.8) | data formatting | bytes 49152
Async XLA Ops:
  1.3 0.7 %copy-start.2 = (s32[8]{0:T(128)S(1)}, s32[8]{0:T(128)}, u32[]{:S(2)}) copy-start(s32[8]{0:T(128)} %match_hbm.1) | copy-start | bytes 100
  2.0 0.7 %copy-start = (bf16[8,768]{1,0:T(8,128)(2,1)S(1)}, bf16[8,768]{1,0:T(8,128)(2,1)}, u32[]{:S(2)}) copy-start(bf16[8,768]{1,0:T(8,128)(2,1)} %images_hbm.1) | copy-start | bytes 36868
  2.7 0.7 %copy-start.1 = (bf16[8,768]{1,0:T(8,128)(2,1)S(1)}, bf16[8,768]{1,0:T(8,128)(2,1)}, u32[]{:S(2)}) copy-start(bf16[8,768]{1,0:T(8,128)(2,1)} %texts_hbm.1) | copy-start | bytes 36868

commit v2 on v1

v2 whole, which is shorter than its diff:
```python
import functools
import jax
import jax.numpy as jnp
from jax import lax
from jax.experimental import pallas as pl
from jax.experimental.pallas import tpu as pltpu
from jax.sharding import PartitionSpec as P

MESH = pl.DeviceIdType.MESH
F32 = jnp.float32
BF16 = jnp.bfloat16


def split_rows(row_count, col_count):
    best = 1
    for low in range(1, row_count + 1):
        if row_count % low == 0:
            if max(low * col_count, row_count // low) < max(best * col_count, row_count // best):
                best = low
    return best


def unit_rows(values):
    wide = values.astype(F32)
    norms = jnp.sqrt(jnp.sum(wide * wide, axis=1, keepdims=True) + 1e-06)
    return (wide / norms, norms)


def back_rows(unit, norms, grads):
    inner = jnp.sum(unit * grads, axis=1, keepdims=True)
    return (grads - unit * inner) / norms


def fold(rows):
    half = rows.shape[1] // 2
    return jnp.concatenate([rows[:, :half], rows[:, half:]], axis=0)


def halves(blocks):
    n, r2, h = blocks.shape
    r = r2 // 2
    wide = blocks.astype(F32)
    return wide[:, :r, :].reshape(n * r, h), wide[:, r:, :].reshape(n * r, h)


def exchange(
    low,
    row_count,
    col_count,
    images_hbm,
    texts_hbm,
    match_hbm,
    scale_hbm,
    bias_hbm,
    grads_ref,
    units_ref,
    norms_ref,
    total_ref,
    images_ref,
    texts_ref,
    match_ref,
    scale_ref,
    bias_ref,
    img_buf,
    txt_buf,
    img_part,
    txt_part,
    img_back,
    txt_back,
    loss_own,
    loss_buf,
    in_sem,
    img_send,
    img_recv,
    txt_send,
    txt_recv,
    ipart_send,
    ipart_recv,
    tpart_send,
    tpart_recv,
    loss_send,
    loss_recv,
):
    shard, width = images_ref.shape
    half = width // 2
    high = row_count // low
    wide = low * col_count
    count = row_count * col_count
    row = lax.axis_index("row")
    col = lax.axis_index("col")
    hi, lo = row // low, row % low
    place = lo * col_count + col

    def at_place(q):
        return {"row": hi * low + q // col_count, "col": q % col_count}

    def at_high(p):
        return {"row": p * low + lo, "col": col}

    barrier = pltpu.get_barrier_semaphore()
    for o in range(1, high):
        pl.semaphore_signal(barrier, inc=1, device_id=at_high((hi + o) % high), device_id_type=MESH)
    for o in range(1, wide):
        pl.semaphore_signal(barrier, inc=1, device_id=at_place((place + o) % wide), device_id_type=MESH)

    loads = [
        pltpu.make_async_copy(src, dst, in_sem.at[n])
        for n, (src, dst) in enumerate(
            [
                (texts_hbm, texts_ref),
                (images_hbm, images_ref),
                (match_hbm, match_ref),
                (scale_hbm, scale_ref),
                (bias_hbm, bias_ref),
            ]
        )
    ]
    for load in loads:
        load.start()
    for load in loads:
        load.wait()
    unit_txt, tnorm = unit_rows(texts_ref[...])
    unit_img, inorm = unit_rows(images_ref[...])
    txt_buf[0] = fold(unit_txt).astype(BF16)
    sub = lax.broadcasted_iota(jnp.int32, (2 * shard, 128), 0)
    index = jnp.zeros((2 * shard, 128), jnp.int32)
    for r in range(shard):
        value = match_ref[r]
        index = jnp.where(sub == r, value // 128, jnp.where(sub == r + shard, value % 128, index))
    img_buf[0] = jnp.concatenate([fold(unit_img), index.astype(F32)], axis=1).astype(BF16)
    scale = scale_ref[0]
    offset = bias_ref[0]

    pl.semaphore_wait(barrier, high + wide - 2)

    first = []
    for o in range(1, high):
        first.append(
            pltpu.make_async_remote_copy(
                txt_buf.at[0], txt_buf.at[o], txt_send.at[o], txt_recv.at[o],
                device_id=at_high((hi + o) % high), device_id_type=MESH,
            )
        )
    for o in range(1, wide):
        first.append(
            pltpu.make_async_remote_copy(
                img_buf.at[0], img_buf.at[o], img_send.at[o], img_recv.at[o],
                device_id=at_place((place + o) % wide), device_id_type=MESH,
            )
        )
    for copy in first:
        copy.start()
    units_ref[0] = unit_img
    units_ref[1] = unit_txt
    norms_ref[0] = jnp.broadcast_to(inorm, (shard, 128))
    norms_ref[1] = jnp.broadcast_to(tnorm, (shard, 128))
    rows, cols = wide * shard, high * shard
    lane = lax.broadcasted_iota(jnp.int32, (rows, cols), 1)
    source = hi - lane // shard
    source = jnp.where(source < 0, source + high, source)
    text_index = ((source * wide + place) * shard + lane % shard).astype(F32)
    for copy in first:
        copy.wait_recv()

    left, right = halves(img_buf[...])
    img_block = jnp.concatenate([left[:, :half], right[:, :half]], axis=1).astype(BF16)
    match_block = left[:, half : half + 1] * 128.0 + right[:, half : half + 1]
    txt_block = jnp.concatenate(halves(txt_buf[...]), axis=1).astype(BF16)
    label = jnp.where(match_block == text_index, F32(1.0), F32(-1.0))
    logits = (
        scale
        * lax.dot_general(img_block, txt_block, (((1,), (1,)), ((), ())), preferred_element_type=F32)
        + offset
    )
    signed = label * logits
    decay = jnp.exp(-jnp.abs(signed))
    coef = (-label * jnp.where(signed >= 0, decay, 1.0) / (1.0 + decay)).astype(BF16)

    def loss_copy(o):
        p = place + o % wide
        p = jnp.where(p >= wide, p - wide, p)
        h = hi + o // wide
        h = jnp.where(h >= high, h - high, h)
        target = {"row": h * low + p // col_count, "col": p % col_count}
        return pltpu.make_async_remote_copy(
            loss_own, loss_buf.at[o], loss_send.at[o], loss_recv.at[o],
            device_id=target, device_id_type=MESH,
        )

    def each_loss(act):
        if count <= 32:
            for o in range(1, count):
                act(loss_copy(o))
        else:
            lax.fori_loop(1, count, lambda o, c: (act(loss_copy(o)), c)[1], 0)

    terms = jnp.minimum(signed, 0.0) - jnp.log1p(decay)
    loss_own[...] = jnp.broadcast_to(jnp.sum(terms, keepdims=True), (1, 128))
    loss_buf[0] = loss_own[...]
    each_loss(lambda copy: copy.start())

    second = []
    txt_terms = lax.dot_general(coef, img_block, (((0,), (0,)), ((), ())), preferred_element_type=F32)
    txt_own = txt_terms[:shard]
    for o in range(1, high):
        txt_part[o] = txt_terms[o * shard : (o + 1) * shard]
        second.append(
            pltpu.make_async_remote_copy(
                txt_part.at[o], txt_back.at[o], tpart_send.at[o], tpart_recv.at[o],
                device_id=at_high((hi + high - o) % high), device_id_type=MESH,
            )
        )
        second[-1].start()
    img_terms = jnp.dot(coef, txt_block, preferred_element_type=F32)
    img_own = img_terms[:shard]
    for o in range(1, wide):
        img_part[o] = img_terms[o * shard : (o + 1) * shard]
        second.append(
            pltpu.make_async_remote_copy(
                img_part.at[o], img_back.at[o], ipart_send.at[o], ipart_recv.at[o],
                device_id=at_place((place + wide - o) % wide), device_id_type=MESH,
            )
        )
        second[-1].start()

    for copy in second:
        copy.wait_recv()

    def gathered(own, back, n):
        for o in range(1, n):
            own = own + back[o]
        return scale * own

    grads_ref[0] = gathered(img_own, img_back, wide)
    grads_ref[1] = gathered(txt_own, txt_back, high)
    each_loss(lambda copy: copy.wait_recv())
    total_ref[...] = jnp.sum(loss_buf[...], axis=0)

    for copy in first + second:
        copy.wait_send()
    each_loss(lambda copy: copy.wait_send())


def finish(pairs, grads_ref, units_ref, norms_ref, total_ref, loss_ref, gimg_ref, gtxt_ref):
    gimg_ref[...] = back_rows(units_ref[0], norms_ref[0][:, :1], grads_ref[0])
    gtxt_ref[...] = back_rows(units_ref[1], norms_ref[1][:, :1], grads_ref[1])
    loss_ref[...] = -total_ref[0, :1] / pairs


def body(images, texts, match, logit_scale, logit_bias):
    row_count = lax.axis_size("row")
    col_count = lax.axis_size("col")
    low = split_rows(row_count, col_count)
    high = row_count // low
    wide = low * col_count
    count = row_count * col_count
    shard, width = images.shape
    half = width // 2
    dma = pltpu.SemaphoreType.DMA
    vmem = pl.BlockSpec(memory_space=pltpu.VMEM)
    inputs = [pltpu.with_memory_space_constraint(images, pltpu.HBM), pltpu.with_memory_space_constraint(texts, pltpu.HBM), pltpu.with_memory_space_constraint(match, pltpu.HBM), logit_scale, logit_bias]
    sums = pl.pallas_call(
        functools.partial(exchange, low, row_count, col_count),
        out_shape=(
            jax.ShapeDtypeStruct((2, shard, width), F32),
            jax.ShapeDtypeStruct((2, shard, width), F32),
            jax.ShapeDtypeStruct((2, shard, 128), F32),
            jax.ShapeDtypeStruct((1, 128), F32),
        ),
        in_specs=[pl.BlockSpec(memory_space=pl.ANY)] * 5,
        out_specs=(vmem,) * 4,
        scratch_shapes=[
            pltpu.VMEM((shard, width), BF16),
            pltpu.VMEM((shard, width), BF16),
            pltpu.SMEM((shard,), jnp.int32),
            pltpu.SMEM((1,), F32),
            pltpu.SMEM((1,), F32),
            pltpu.VMEM((wide, 2 * shard, half + 128), BF16),
            pltpu.VMEM((high, 2 * shard, half), BF16),
            pltpu.VMEM((wide, shard, width), F32),
            pltpu.VMEM((high, shard, width), F32),
            pltpu.VMEM((wide, shard, width), F32),
            pltpu.VMEM((high, shard, width), F32),
            pltpu.VMEM((1, 128), F32),
            pltpu.VMEM((count, 1, 128), F32),
            dma((5,)),
            dma((wide,)),
            dma((wide,)),
            dma((high,)),
            dma((high,)),
            dma((wide,)),
            dma((wide,)),
            dma((high,)),
            dma((high,)),
            dma((count,)),
            dma((count,)),
        ],
        compiler_params=pltpu.CompilerParams(
            collective_id=0, has_side_effects=True, vmem_limit_bytes=32 * 1024 * 1024
        ),
    )(*inputs)
    return tuple(
        pl.pallas_call(
            functools.partial(finish, shard * count),
            out_shape=(
                jax.ShapeDtypeStruct((1,), F32),
                jax.ShapeDtypeStruct((shard, width), F32),
                jax.ShapeDtypeStruct((shard, width), F32),
            ),
            in_specs=[vmem] * 4,
            out_specs=(vmem,) * 3,
            compiler_params=pltpu.CompilerParams(vmem_limit_bytes=4 * 1024 * 1024),
        )(*sums)
    )


def solution(mesh):
    placed = (
        P(("grp", "row", "col"), None),
        P(("grp", "row", "col"), None),
        P(("grp", "row", "col")),
        P(),
        P(),
    )
    return jax.shard_map(
        body,
        mesh=mesh,
        in_specs=placed,
        out_specs=(P("grp"), P(("grp", "row", "col"), None), P(("grp", "row", "col"), None)),
        check_vma=False,
    )
```

time: 22.6 us -> 17.2 us (0.76)
  local copies, waits for them, and re-layouts: 2.63 us -> 0 us
  between operations: 3.71 us -> 1.93 us
  Pallas kernels: 15.9 us -> 15 us
    unnamed x8 -> x0, local copies, waits for them, and re-layouts: 2.63 us -> none
    pallas_call x1 -> x2, Pallas kernels: 15.9 us -> 15 us  [the longest x1 14.3 us: body(): pl.pallas_call(functools.partial(exchange, low, row_count, col_count), ou...]
where the time goes in v2:
time: 17.2 us; the launch traced here: 17 us
  Pallas kernels  15 us (87%)
  between operations  1.93 us (11%)
    pallas_call x1, Pallas kernels, body(): pl.pallas_call(functools.partial(exchange, low, row_count, col_count), ou...  14.3 us
    pallas_call x1, Pallas kernels, body(): pl.pallas_call(functools.partial(finish, shard * count), out_shape=(jax.S...  0.73 us

profile of v2, /device:TPU:0, one launch (start us, length us, event | category | flops | bytes accessed | tf_op | source)
XLA Modules:
  0.0 17.0 jit_solution(466630960933555702)
XLA Ops:
  1.9 14.3 %shard_map.76 = (f32[2,8,768]{2,1,0:T(8,128)S(1)}, f32[2,8,768]{2,1,0:T(8,128)S(1)}, f32[2,8,128]{2,1,0:T(8,128)S(1)}, f32[1,128]{1,0:T(1,128)S(1)}) custom-call(bf16[8,768]{1,0:T(8,128)(2,1)} %images_hbm.1, bf16[8,768]{1,0:T(8,128)(2,1)} %texts_hbm.1, s32[8]{0:T(128)} %match_hbm.1, f32[1]{0:T(128)S(6)} %copy.8.scale_hbm, f32[1]{0:T(128)S(6)} %copy.9.bias_hbm), custom_call_target="tpu_custom_call" | custom-call | tf_op jit(solution)/shard_map/pallas_call | solution.py:262
  16.3 0.7 %shard_map.77 = (f32[1]{0:T(128)}, f32[8,768]{1,0:T(8,128)}, f32[8,768]{1,0:T(8,128)}) custom-call(f32[2,8,768]{2,1,0:T(8,128)S(1)} %get-tuple-element.7.grads_ref, f32[2,8,768]{2,1,0:T(8,128)S(1)} %get-tuple-element.8.units_ref, f32[2,8,128]{2,1,0:T(8,128)S(1)} %get-tuple-element.9.norms_ref, f32[1,128]{1,0:T(1,128)S(1)} %get-tuple-element.10.total_ref), custom_call_target="tpu_custom_call" | custom-call | tf_op jit(solution)/shard_map/pallas_call | solution.py:303

commit v3 on v2

--- a/solution.py
+++ b/solution.py
@@ -15,7 +15,7 @@
     best = 1
     for low in range(1, row_count + 1):
         if row_count % low == 0:
-            if max(low * col_count, row_count // low) < max(best * col_count, row_count // best):
+            if max(low, row_count // low * col_count) < max(best, row_count // best * col_count):
                 best = low
     return best
 
@@ -83,25 +83,25 @@
 ):
     shard, width = images_ref.shape
     half = width // 2
-    high = row_count // low
-    wide = low * col_count
+    high = row_count // low * col_count
+    wide = low
     count = row_count * col_count
     row = lax.axis_index("row")
     col = lax.axis_index("col")
     hi, lo = row // low, row % low
-    place = lo * col_count + col
+    level = hi * col_count + col
 
     def at_place(q):
-        return {"row": hi * low + q // col_count, "col": q % col_count}
+        return {"row": hi * low + q, "col": col}
 
     def at_high(p):
-        return {"row": p * low + lo, "col": col}
+        return {"row": p // col_count * low + lo, "col": p % col_count}
 
     barrier = pltpu.get_barrier_semaphore()
     for o in range(1, high):
-        pl.semaphore_signal(barrier, inc=1, device_id=at_high((hi + o) % high), device_id_type=MESH)
+        pl.semaphore_signal(barrier, inc=1, device_id=at_high((level + o) % high), device_id_type=MESH)
     for o in range(1, wide):
-        pl.semaphore_signal(barrier, inc=1, device_id=at_place((place + o) % wide), device_id_type=MESH)
+        pl.semaphore_signal(barrier, inc=1, device_id=at_place((lo + o) % wide), device_id_type=MESH)
 
     loads = [
         pltpu.make_async_copy(src, dst, in_sem.at[n])
@@ -138,14 +138,14 @@
         first.append(
             pltpu.make_async_remote_copy(
                 txt_buf.at[0], txt_buf.at[o], txt_send.at[o], txt_recv.at[o],
-                device_id=at_high((hi + o) % high), device_id_type=MESH,
+                device_id=at_high((level + o) % high), device_id_type=MESH,
             )
         )
     for o in range(1, wide):
         first.append(
             pltpu.make_async_remote_copy(
                 img_buf.at[0], img_buf.at[o], img_send.at[o], img_recv.at[o],
-                device_id=at_place((place + o) % wide), device_id_type=MESH,
+                device_id=at_place((lo + o) % wide), device_id_type=MESH,
             )
         )
     for copy in first:
@@ -156,9 +156,10 @@
     norms_ref[1] = jnp.broadcast_to(tnorm, (shard, 128))
     rows, cols = wide * shard, high * shard
     lane = lax.broadcasted_iota(jnp.int32, (rows, cols), 1)
-    source = hi - lane // shard
+    source = level - lane // shard
     source = jnp.where(source < 0, source + high, source)
-    text_index = ((source * wide + place) * shard + lane % shard).astype(F32)
+    text_index = (source // col_count * low + lo) * col_count + source % col_count
+    text_index = (text_index * shard + lane % shard).astype(F32)
     for copy in first:
         copy.wait_recv()
 
@@ -177,11 +178,11 @@
     coef = (-label * jnp.where(signed >= 0, decay, 1.0) / (1.0 + decay)).astype(BF16)
 
     def loss_copy(o):
-        p = place + o % wide
+        p = lo + o % wide
         p = jnp.where(p >= wide, p - wide, p)
-        h = hi + o // wide
+        h = level + o // wide
         h = jnp.where(h >= high, h - high, h)
-        target = {"row": h * low + p // col_count, "col": p % col_count}
+        target = {"row": h // col_count * low + p, "col": h % col_count}
         return pltpu.make_async_remote_copy(
             loss_own, loss_buf.at[o], loss_send.at[o], loss_recv.at[o],
             device_id=target, device_id_type=MESH,
@@ -207,7 +208,7 @@
         second.append(
             pltpu.make_async_remote_copy(
                 txt_part.at[o], txt_back.at[o], tpart_send.at[o], tpart_recv.at[o],
-                device_id=at_high((hi + high - o) % high), device_id_type=MESH,
+                device_id=at_high((level + high - o) % high), device_id_type=MESH,
             )
         )
         second[-1].start()
@@ -218,7 +219,7 @@
         second.append(
             pltpu.make_async_remote_copy(
                 img_part.at[o], img_back.at[o], ipart_send.at[o], ipart_recv.at[o],
-                device_id=at_place((place + wide - o) % wide), device_id_type=MESH,
+                device_id=at_place((lo + wide - o) % wide), device_id_type=MESH,
             )
         )
         second[-1].start()
@@ -251,8 +252,8 @@
     row_count = lax.axis_size("row")
     col_count = lax.axis_size("col")
     low = split_rows(row_count, col_count)
-    high = row_count // low
-    wide = low * col_count
+    high = row_count // low * col_count
+    wide = low
     count = row_count * col_count
     shard, width = images.shape
     half = width // 2

time: 17.2 us -> 16.6 us (0.965)
  Pallas kernels: 15 us -> 14.4 us
    pallas_call x1, Pallas kernels: 14.3 us -> 13.7 us  [body(): pl.pallas_call(functools.partial(exchange, low, row_count, col_count), ou...]
where the time goes in v3:
time: 16.6 us; the launch traced here: 16.4 us
  Pallas kernels  14.4 us (87%)
  between operations  1.93 us (12%)
    pallas_call x1, Pallas kernels, body(): pl.pallas_call(functools.partial(exchange, low, row_count, col_count), ou...  13.7 us
    pallas_call x1, Pallas kernels, body(): pl.pallas_call(functools.partial(finish, shard * count), out_shape=(jax.S...  0.73 us

profile of v3, /device:TPU:0, one launch (start us, length us, event | category | flops | bytes accessed | tf_op | source)
XLA Modules:
  0.0 16.4 jit_solution(7527159427283379389)
XLA Ops:
  1.9 13.7 %shard_map.76 = (f32[2,8,768]{2,1,0:T(8,128)S(1)}, f32[2,8,768]{2,1,0:T(8,128)S(1)}, f32[2,8,128]{2,1,0:T(8,128)S(1)}, f32[1,128]{1,0:T(1,128)S(1)}) custom-call(bf16[8,768]{1,0:T(8,128)(2,1)} %images_hbm.1, bf16[8,768]{1,0:T(8,128)(2,1)} %texts_hbm.1, s32[8]{0:T(128)} %match_hbm.1, f32[1]{0:T(128)S(6)} %copy.8.scale_hbm, f32[1]{0:T(128)S(6)} %copy.9.bias_hbm), custom_call_target="tpu_custom_call" | custom-call | tf_op jit(solution)/shard_map/pallas_call | solution.py:263
  15.6 0.7 %shard_map.77 = (f32[1]{0:T(128)}, f32[8,768]{1,0:T(8,128)}, f32[8,768]{1,0:T(8,128)}) custom-call(f32[2,8,768]{2,1,0:T(8,128)S(1)} %get-tuple-element.7.grads_ref, f32[2,8,768]{2,1,0:T(8,128)S(1)} %get-tuple-element.8.units_ref, f32[2,8,128]{2,1,0:T(8,128)S(1)} %get-tuple-element.9.norms_ref, f32[1,128]{1,0:T(1,128)S(1)} %get-tuple-element.10.total_ref), custom_call_target="tpu_custom_call" | custom-call | tf_op jit(solution)/shard_map/pallas_call | solution.py:304

commit v4 on v3

--- a/solution.py
+++ b/solution.py
@@ -18,6 +18,10 @@
             if max(low, row_count // low * col_count) < max(best, row_count // best * col_count):
                 best = low
     return best
+
+
+def far_first(n):
+    return sorted(range(1, n), key=lambda o: abs(o - n // 2))
 
 
 def unit_rows(values):
@@ -134,14 +138,14 @@
     pl.semaphore_wait(barrier, high + wide - 2)
 
     first = []
-    for o in range(1, high):
+    for o in far_first(high):
         first.append(
             pltpu.make_async_remote_copy(
                 txt_buf.at[0], txt_buf.at[o], txt_send.at[o], txt_recv.at[o],
                 device_id=at_high((level + o) % high), device_id_type=MESH,
             )
         )
-    for o in range(1, wide):
+    for o in far_first(wide):
         first.append(
             pltpu.make_async_remote_copy(
                 img_buf.at[0], img_buf.at[o], img_send.at[o], img_recv.at[o],
@@ -203,7 +207,7 @@
     second = []
     txt_terms = lax.dot_general(coef, img_block, (((0,), (0,)), ((), ())), preferred_element_type=F32)
     txt_own = txt_terms[:shard]
-    for o in range(1, high):
+    for o in far_first(high):
         txt_part[o] = txt_terms[o * shard : (o + 1) * shard]
         second.append(
             pltpu.make_async_remote_copy(
@@ -214,7 +218,7 @@
         second[-1].start()
     img_terms = jnp.dot(coef, txt_block, preferred_element_type=F32)
     img_own = img_terms[:shard]
-    for o in range(1, wide):
+    for o in far_first(wide):
         img_part[o] = img_terms[o * shard : (o + 1) * shard]
         second.append(
             pltpu.make_async_remote_copy(
@@ -224,16 +228,18 @@
         )
         second[-1].start()
 
-    for copy in second:
-        copy.wait_recv()
 
     def gathered(own, back, n):
         for o in range(1, n):
             own = own + back[o]
         return scale * own
 
+    for copy in second[: high - 1]:
+        copy.wait_recv()
+    grads_ref[1] = gathered(txt_own, txt_back, high)
+    for copy in second[high - 1 :]:
+        copy.wait_recv()
     grads_ref[0] = gathered(img_own, img_back, wide)
-    grads_ref[1] = gathered(txt_own, txt_back, high)
     each_loss(lambda copy: copy.wait_recv())
     total_ref[...] = jnp.sum(loss_buf[...], axis=0)
 

time: 16.6 us -> 16.6 us (level)
  no operation moved by 1% of the time
where the time goes in v4:
time: 16.6 us; the launch traced here: 16.4 us
  Pallas kernels  14.4 us (87%)
  between operations  1.93 us (12%)
    pallas_call x1, Pallas kernels, body(): pl.pallas_call(functools.partial(exchange, low, row_count, col_count), ou...  13.7 us
    pallas_call x1, Pallas kernels, body(): pl.pallas_call(functools.partial(finish, shard * count), out_shape=(jax.S...  0.73 us

profile of v4, /device:TPU:0, one launch (start us, length us, event | category | flops | bytes accessed | tf_op | source)
XLA Modules:
  0.0 16.4 jit_solution(14350081769452428558)
XLA Ops:
  1.9 13.7 %shard_map.76 = (f32[2,8,768]{2,1,0:T(8,128)S(1)}, f32[2,8,768]{2,1,0:T(8,128)S(1)}, f32[2,8,128]{2,1,0:T(8,128)S(1)}, f32[1,128]{1,0:T(1,128)S(1)}) custom-call(bf16[8,768]{1,0:T(8,128)(2,1)} %images_hbm.1, bf16[8,768]{1,0:T(8,128)(2,1)} %texts_hbm.1, s32[8]{0:T(128)} %match_hbm.1, f32[1]{0:T(128)S(6)} %copy.8.scale_hbm, f32[1]{0:T(128)S(6)} %copy.9.bias_hbm), custom_call_target="tpu_custom_call" | custom-call | tf_op jit(solution)/shard_map/pallas_call | solution.py:269
  15.6 0.7 %shard_map.77 = (f32[1]{0:T(128)}, f32[8,768]{1,0:T(8,128)}, f32[8,768]{1,0:T(8,128)}) custom-call(f32[2,8,768]{2,1,0:T(8,128)S(1)} %get-tuple-element.7.grads_ref, f32[2,8,768]{2,1,0:T(8,128)S(1)} %get-tuple-element.8.units_ref, f32[2,8,128]{2,1,0:T(8,128)S(1)} %get-tuple-element.9.norms_ref, f32[1,128]{1,0:T(1,128)S(1)} %get-tuple-element.10.total_ref), custom_call_target="tpu_custom_call" | custom-call | tf_op jit(solution)/shard_map/pallas_call | solution.py:310
